TPU v7x, 32 devices: a whole 2x2x4 slice. The times are simulated.
32 devices in a mesh: dp: 4 (over z), bank: 4 (over y, x), head: 2 (over core).
Axes of the slice: x: 2, y: 2, z: 4, core: 2. Of those that a mesh axis runs over, the one named last changes fastest.
Arguments:
- feats: bfloat16 [2048, 2048], P('dp'), may hold values from -6 to 6
- w_first: bfloat16 [2048, 2048], P(None, ('bank', 'head')), may hold values from -0.125 to 0.125
- w_second: bfloat16 [2048, 256], P(('bank', 'head')), may hold values from -0.125 to 0.125
- fresh_keys: float32 [2048, 256], P('dp'), may hold values from -6 to 6
- bank: float32 [32768, 256], P(('bank', 'head'))
- block_lists: int32 [4, 32], P('dp'), may hold values from 0 to 63, as said below
- dest_rows: int32 [2048], P('dp'), may hold values from 0 to 32767, as said below
Outputs:
- loss: float32 [2048], P('dp')
- grad_first: float32 [2048, 2048], P('dp', ('bank', 'head'))
- grad_second: float32 [2048, 256], P(('bank', 'head'))
- new_bank: float32 [32768, 256], P(('bank', 'head'))
Inputs may be any that keep to these rules, and one draw needn't show every extreme that they name: `block_lists`: each row names 32 different blocks. `dest_rows`: all entries differ; the 512 entries of query block g name exactly 64 rows in each range of rows o * 4096 to (o + 1) * 4096 - 1.
All inputs are finite; a program needn't handle non-finite values.
Results may differ from a plain program's by a relative error of at most 0.012.
Values sent between devices are 32-bit elements; how exact they have to be, the bound alone decides.
A program may use at most 128 MiB of HBM per device.

v0:
```python
import jax
import jax.numpy as jnp
from jax import lax
from jax.sharding import PartitionSpec as P

BLOCK = 512
sharpness_divisor = 0.2
epsilon = 1e-06
lowest = -1e30


def joined(array, axis, combine):
    everything = jax.tree.map(lambda part: lax.all_gather(part, axis), array)
    leading = jax.tree.map(lambda part: part[0], everything)

    def hop(k, so_far):
        return combine(so_far, jax.tree.map(lambda part: part[k], everything))

    return lax.fori_loop(1, lax.axis_size(axis), hop, leading)


def unit_rows(values):
    norms = jnp.sqrt(jnp.sum(values * values, axis=1, keepdims=True) + epsilon)
    return (values / norms, norms)


def exact_scores(anchor_matrix, bank_entries):
    return (
        lax.dot_general(
            anchor_matrix,
            bank_entries,
            (((1,), (1,)), ((), ())),
            precision=lax.Precision.HIGHEST,
            preferred_element_type=jnp.float32,
        )
        / sharpness_divisor
    )


def join_stats(first, second):
    best = jnp.maximum(first[0], second[0])
    partition_total = first[1] * jnp.exp(first[0] - best) + second[1] * jnp.exp(second[0] - best)
    return (best, partition_total)


def shards(feats, w_first, w_second, fresh_keys, bank, block_lists, dest_rows):
    owner = lax.axis_index(("bank", "head"))
    owner_rows = bank.shape[0]
    hidden = jnp.maximum(jnp.dot(feats, w_first, preferred_element_type=jnp.float32), 0.0).astype(
        jnp.bfloat16
    )
    partial_embed = jnp.dot(hidden, w_second, preferred_element_type=jnp.float32)
    embed = lax.psum(partial_embed, ("bank", "head"))
    anchor_matrix, norms = unit_rows(embed)
    unit_length_bank, unused = unit_rows(fresh_keys)
    matching_similarity = jnp.sum(anchor_matrix * unit_length_bank, axis=1) / sharpness_divisor
    listed = block_lists[0]
    blocks_here = owner_rows // BLOCK
    owned = listed // blocks_here == owner
    owned_count = jnp.sum(owned.astype(jnp.int32))
    order = jnp.argsort(jnp.where(owned, 0, 1).astype(jnp.int32), stable=True)
    local_blocks = listed[order] - owner * blocks_here
    row_count = anchor_matrix.shape[0]

    def block_keys(index):
        return lax.dynamic_slice_in_dim(bank, local_blocks[index] * BLOCK, BLOCK, 0)

    start_best = jnp.full((row_count,), lowest, jnp.float32)
    start_total = jnp.zeros((row_count,), jnp.float32)
    start_weighted = jnp.zeros((row_count, anchor_matrix.shape[1]), jnp.float32)

    def first_pass(index, carry):
        best, partition_total = carry
        similarity_matrix = exact_scores(anchor_matrix, block_keys(index))
        new_best = jnp.maximum(best, jnp.max(similarity_matrix, axis=1))
        partition_total = partition_total * jnp.exp(best - new_best) + jnp.sum(
            jnp.exp(similarity_matrix - new_best[:, None]), axis=1
        )
        return (new_best, partition_total)

    local_stats = lax.fori_loop(0, owned_count, first_pass, (start_best, start_total))
    neg_best, neg_total = joined(local_stats, ("bank", "head"), join_stats)
    best = jnp.maximum(neg_best, matching_similarity)
    positive_weight = jnp.exp(matching_similarity - best)
    partition_total = neg_total * jnp.exp(neg_best - best) + positive_weight

    def second_pass(index, probability_mixed_bank):
        bank_entries = block_keys(index)
        shares = (
            jnp.exp(exact_scores(anchor_matrix, bank_entries) - best[:, None])
            / partition_total[:, None]
        )
        return probability_mixed_bank + jnp.dot(
            shares,
            bank_entries,
            precision=lax.Precision.HIGHEST,
            preferred_element_type=jnp.float32,
        )

    local_weighted = lax.fori_loop(0, owned_count, second_pass, start_weighted)
    probability_mixed_bank = lax.psum(local_weighted, ("bank", "head"))
    loss = best + jnp.log(partition_total) - matching_similarity
    anchor_derivative = (
        probability_mixed_bank
        + (positive_weight / partition_total - 1.0)[:, None] * unit_length_bank
    ) / sharpness_divisor
    inner = jnp.sum(anchor_matrix * anchor_derivative, axis=1, keepdims=True)
    grad_z = ((anchor_derivative - anchor_matrix * inner) / norms).astype(jnp.bfloat16)
    second_part = lax.dot_general(
        hidden, grad_z, (((0,), (0,)), ((), ())), preferred_element_type=jnp.float32
    )
    grad_second = lax.psum(second_part, "dp")
    grad_hidden = lax.dot_general(
        grad_z, w_second, (((1,), (1,)), ((), ())), preferred_element_type=jnp.float32
    )
    grad_pre = jnp.where(hidden > 0, grad_hidden, 0.0).astype(jnp.bfloat16)
    grad_first = lax.psum_scatter(
        lax.dot_general(
            feats, grad_pre, (((0,), (0,)), ((), ())), preferred_element_type=jnp.float32
        ),
        "dp",
        scatter_dimension=0,
        tiled=True,
    )
    got_keys, got_dest = (
        lax.all_gather(unit_length_bank, "dp", axis=0, tiled=True),
        lax.all_gather(dest_rows.astype(jnp.float32), "dp", axis=0, tiled=True),
    )
    local_rows = got_dest.astype(jnp.int32) - owner * owner_rows
    inside = (local_rows >= 0) & (local_rows < owner_rows)
    new_bank = bank.at[jnp.where(inside, local_rows, owner_rows)].set(got_keys, mode="drop")
    return (loss, grad_first, grad_second, new_bank)


def solution(mesh):
    return jax.shard_map(
        shards,
        mesh=mesh,
        in_specs=(
            P("dp", None),
            P(None, ("bank", "head")),
            P(("bank", "head"), None),
            P("dp", None),
            P(("bank", "head"), None),
            P("dp", None),
            P("dp"),
        ),
        out_specs=(
            P("dp"),
            P("dp", ("bank", "head")),
            P(("bank", "head"), None),
            P(("bank", "head"), None),
        ),
        check_vma=False,
    )
```

profile of v0, /device:TPU:0, one launch (start us, length us, event | category | flops | bytes accessed | tf_op | source)
XLA Modules:
  0.0 383.6 jit_solution(11246029741084995186)
XLA Ops:
  7.2 4.6 %copy.49 = f32[4096,256]{1,0:T(8,128)} copy(f32[4096,256]{1,0:T(8,128)} %param.17) | data formatting | bytes 8388608
  17.1 54.1 %all-reduce.4.cloned.1.call-done = f32[512,256]{1,0:T(8,128)} async-done(((f32[512,256]{1,0:T(8,128)}), f32[512,256]{1,0:T(8,128)}) %all-reduce.4.cloned.1.call-update) | async-done | bytes 524304 | tf_op jit(solution)/shard_map/psum | solution.py:53
  74.5 36.0 %while.39 = (s32[]{:T(128)}, f32[512]{0:T(512)S(1)}, f32[512]{0:T(512)S(1)}, s32[]{:T(128)}, s32[32]{0:T(128)S(1)}, /*index=5*/f32[4096,256]{1,0:T(8,128)}, f32[...) while((s32[]{:T(128)}, f32[512]{0:T(512)S(1)}, ...), condition=%wide.region_7.8_spmd, body=%wide.region_4.0_spmd.sunk | while | flops 806355968 | bytes 3172573 | solution.py:81
  110.5 7.4 %all-gather.2 = f32[8,1,512]{2,1,0:T(1,128)S(1)} all-gather(f32[1,1,512]{2,1,0:T(1,128)S(1)} %bitcast.49), channel_id=2, replica_groups=mesh['dp'=4,'bank'=4,'head'=2] {'bank','head'}, dimensions={0}, use_global_device_ids=true | all-gather | bytes 18432 | tf_op jit(solution)/shard_map/all_gather | solution.py:13
  118.0 9.4 %all-gather.3 = f32[8,1,512]{2,1,0:T(1,128)S(1)} all-gather(f32[1,1,512]{2,1,0:T(1,128)S(1)} %bitcast.52), channel_id=3, replica_groups=mesh['dp'=4,'bank'=4,'head'=2] {'bank','head'}, dimensions={0}, use_global_device_ids=true | all-gather | bytes 18432 | tf_op jit(solution)/shard_map/all_gather | solution.py:13
  128.4 62.4 %while.41 = (s32[]{:T(128)}, f32[512,256]{1,0:T(8,128)S(1)}, s32[]{:T(128)}, s32[32]{0:T(128)}, f32[4096,256]{1,0:T(8,128)}, /*index=5*/f32[512,256]{1,0:T(8,128...) while((s32[]{:T(128)}, f32[512,256]{1,0:T(8,128)S(1)}, ...), condition=%wide.region_13.14_spmd, body=%wide.region_12.13_spmd.sunk | while | flops 1611530240 | bytes 4722921 | solution.py:100
  130.9 2.2 fusion.45
  133.1 3.0 convolution_add_fusion.2
  140.8 3.0 convolution_add_fusion.2
  148.5 3.0 convolution_add_fusion.2
  154.1 2.2 fusion.45
  156.3 3.0 convolution_add_fusion.2
  164.0 3.0 convolution_add_fusion.2
  169.5 2.2 fusion.45
  171.7 3.0 convolution_add_fusion.2
  179.4 3.0 convolution_add_fusion.2
  187.1 3.0 convolution_add_fusion.2
  192.4 52.9 %all-reduce.6.cloned.1.call-done = f32[512,256]{1,0:T(8,128)} async-done(((f32[512,256]{1,0:T(8,128)}), f32[512,256]{1,0:T(8,128)}) %all-reduce.6.cloned.1.call-update) | async-done | bytes 524304 | tf_op jit(solution)/shard_map/psum | solution.py:101
  248.8 3.3 convolution_bitcast_fusion
  252.8 12.1 %all-gather.4 = f32[4,1,512]{2,1,0:T(1,128)S(1)} all-gather(f32[1,1,512]{2,1,0:T(1,128)S(1)} %bitcast.58), channel_id=1, replica_groups=mesh['dp'=4,'bank'=4,'head'=2] {'dp'}, dimensions={0}, use_global_device_ids=true | all-gather | bytes 10240 | tf_op jit(solution)/shard_map/all_gather | solution.py:127
  265.9 27.0 %all-gather.7.cloned.1.call-done = f32[2048,256]{1,0:T(8,128)} async-done(((f32[512,256]{1,0:T(8,128)}), f32[2048,256]{1,0:T(8,128)}) %all-gather.7.cloned.1.call-update) | async-done | bytes 2097168 | tf_op jit(solution)/shard_map/all_gather | solution.py:126
  292.9 13.6 %scatter_fusion = f32[4096,256]{1,0:T(8,128)} fusion(f32[4096,256]{1,0:T(8,128)} %get-tuple-element.541, s32[2048]{0:T(1024)S(1)} %compare_select_fusion, f32[2048,256]{1,0:T(8,128)} %all-gather.7.cloned.1.call-done), kind=kCustom, calls=%fused_computation.1 | custom fusion | bytes 6299648 | tf_op jit(solution)/shard_map/scatter | solution.py:131
  306.5 31.3 %reduce-scatter.2.cloned.1.call-done = f32[512,256]{0,1:T(8,128)} async-done(((f32[2048,256]{0,1:T(8,128)}), f32[512,256]{0,1:T(8,128)}) %reduce-scatter.2.cloned.1.call-update) | async-done | bytes 524304 | tf_op jit(solution)/shard_map/reduce_scatter | solution.py:117
  339.9 35.6 %all-reduce.8.cloned.1.call-done = f32[256,256]{1,0:T(8,128)} async-done(((f32[256,256]{1,0:T(8,128)}), f32[256,256]{1,0:T(8,128)}) %all-reduce.8.cloned.1.call-update) | async-done | bytes 262160 | tf_op jit(solution)/shard_map/psum | solution.py:112
  (136 shorter events, 65.0 us)
Async XLA Ops:
  7.2 4.7 %copy-start = (bf16[512,2048]{1,0:T(8,128)(2,1)S(1)}, bf16[512,2048]{1,0:T(8,128)(2,1)}, u32[]{:S(2)}) copy-start(bf16[512,2048]{1,0:T(8,128)(2,1)} %param.13) | copy-start | bytes 6291460
  7.2 64.1 %all-reduce.4.cloned.1.call-start = ((), (), s32[]{:S(2)}) async-start(), calls=%async_computation.1 | async-start | bytes 1048576 | tf_op jit(solution)/shard_map/psum | solution.py:53
  7.2 4.6 %copy-start.9 = (bf16[2048,256]{1,0:T(8,128)(2,1)S(1)}, bf16[2048,256]{1,0:T(8,128)(2,1)}, u32[]{:S(2)}) copy-start(bf16[2048,256]{1,0:T(8,128)(2,1)} %param.14) | copy-start | bytes 3145732
  11.9 0.9 copy-start.6
  11.9 2.0 copy-start.1
  11.9 5.1 %copy-start.5 = (f32[512,256]{1,0:T(8,128)S(1)}, f32[512,256]{1,0:T(8,128)}, u32[]{:S(2)}) copy-start(f32[512,256]{1,0:T(8,128)} %param.16) | copy-start | bytes 1572868
  13.8 231.5 %all-reduce.6.cloned.1.call-start = ((), (), s32[]{:S(2)}) async-start(), calls=%async_computation.2 | async-start | bytes 1048576 | tf_op jit(solution)/shard_map/psum | solution.py:101
  110.5 17.2 %copy-start.8 = (s32[32]{0:T(128)}, s32[32]{0:T(128)S(1)}, u32[]{:S(2)}) copy-start(s32[32]{0:T(128)S(1)} %get-tuple-element.559) | copy-start | bytes 388
  190.8 0.8 copy-start.2
  191.6 55.2 %copy-start.3 = (f32[512,256]{1,0:T(8,128)S(1)}, f32[512,256]{1,0:T(8,128)}, u32[]{:S(2)}) copy-start(f32[512,256]{1,0:T(8,128)} %get-tuple-element.283) | copy-start | bytes 1572868
  191.6 101.3 %all-gather.7.cloned.1.call-start = ((), (), s32[]{:S(2)}) async-start(), calls=%async_computation.5 | async-start | bytes 2621440 | tf_op jit(solution)/shard_map/all_gather | solution.py:126
  192.4 145.5 %reduce-scatter.2.cloned.1.call-start = ((), (), s32[]{:S(2)}) async-start(), calls=%async_computation.3 | async-start | bytes 2621440 | tf_op jit(solution)/shard_map/reduce_scatter | solution.py:117
  252.1 0.7 copy-start.7
  252.1 12.8 %copy-start.4 = (bf16[512,256]{1,0:T(8,128)(2,1)S(1)}, bf16[512,256]{1,0:T(8,128)(2,1)}, u32[]{:S(2)}) copy-start(bf16[512,256]{1,0:T(8,128)(2,1)} %divide_convert_fusion) | copy-start | bytes 786436
  252.2 123.3 %all-reduce.8.cloned.1.call-start = ((), (), s32[]{:S(2)}) async-start(), calls=%async_computation.4 | async-start | bytes 524288 | tf_op jit(solution)/shard_map/psum | solution.py:112
Sparse Core Ops, SparseCore 0:
  13.9 57.2 all-reduce.3
  191.8 53.5 all-reduce.5
  247.5 45.3 all-gather.6
  295.1 42.7 reduce-scatter.1
  340.7 34.6 all-reduce.7
where the time goes:
time: 386 us; the launch traced here: 384 us
  waiting for transfers between devices  202 us (52%)
  matrix products  64.2 us (17%)
  local copies, waits for them, and re-layouts  39.8 us (10%)
  blocking collectives  28.9 us (7%)
  loops' own time  23.3 us (6%)
  between operations  14 us (4%)
  other arithmetic  11.7 us (3%)
    psum x1, waiting for transfers between devices, shards(): embed = lax.psum(partial_embed, ('bank', 'head'))  54.1 us
    psum x1, waiting for transfers between devices, shards(): probability_mixed_bank = lax.psum(local_weighted, ('bank', 'head'))  52.9 us
    psum x1, waiting for transfers between devices, shards(): grad_second = lax.psum(second_part, 'dp')  35.6 us
    dot_general x16, matrix products, exact_scores(): lax.dot_general(anchor_matrix, bank_entries, (((1,), (1,)), ((), ())), pr...  34.4 us
    reduce_scatter x1, waiting for transfers between devices, shards(): lax.psum_scatter(lax.dot_general(feats, grad_pre, (((0,), (0,)), ((), ())...  31.3 us
    all_gather x1, waiting for transfers between devices, shards(): lax.all_gather(unit_length_bank, 'dp', axis=0, tiled=True)  27 us
    dot_general x8, matrix products, second_pass(): jnp.dot(shares, bank_entries, precision=lax.Precision.HIGHEST, preferred_...  23.8 us
    all_gather x2, blocking collectives, joined(): everything = jax.tree.map(lambda part: lax.all_gather(part, axis), array)  16.8 us
  transfers between devices with their start and end apart: 5, of which 5 were waited for; matrix products, arithmetic and copies ran while one was open for 7% of the time, Pallas kernels for 0%

commit v1 on v0

--- a/solution.py
+++ b/solution.py
@@ -7,6 +7,19 @@
 sharpness_divisor = 0.2
 epsilon = 1e-06
 lowest = -1e30
+
+
+def ring_gather(x, axis, dim):
+    ways = lax.axis_size(axis)
+    up = [(d, (d + 1) % ways) for d in range(ways)]
+    down = [(d, (d - 1) % ways) for d in range(ways)]
+    earlier, later = ([x], [x])
+    for _ in range(ways // 2):
+        earlier.append(lax.ppermute(earlier[-1], axis, up))
+    for _ in range((ways - 1) // 2):
+        later.append(lax.ppermute(later[-1], axis, down))
+    line = jnp.concatenate([*earlier[::-1], *later[1:]], axis=dim)
+    return jnp.roll(line, (lax.axis_index(axis) - ways // 2) * x.shape[dim], axis=dim)
 
 
 def joined(array, axis, combine):
@@ -123,7 +136,7 @@
         tiled=True,
     )
     got_keys, got_dest = (
-        lax.all_gather(unit_length_bank, "dp", axis=0, tiled=True),
+        ring_gather(unit_length_bank, "dp", 0),
         lax.all_gather(dest_rows.astype(jnp.float32), "dp", axis=0, tiled=True),
     )
     local_rows = got_dest.astype(jnp.int32) - owner * owner_rows

time: 386 us -> 357 us (0.925)
  waiting for transfers between devices: 202 us -> 160 us
  local copies, waits for them, and re-layouts: 39.8 us -> 51.8 us
    all_gather x1 -> x0, waiting for transfers between devices: 27 us -> none  [shards(): lax.all_gather(unit_length_bank, 'dp', axis=0, tiled=True)]
    reduce_scatter x1, waiting for transfers between devices: 31.3 us -> 14.9 us  [shards(): lax.psum_scatter(lax.dot_general(feats, grad_pre, (((0,), (0,)), ((), ())...]
    ppermute x0 -> x3, waiting for transfers between devices: none -> 12.1 us  [the longest x2 12.1 us: ring_gather(): earlier.append(lax.ppermute(earlier[-1], axis, up))]
    unnamed x25 -> x27, local copies, waits for them, and re-layouts: 9.96 us -> 20.5 us
    psum x1, waiting for transfers between devices: 52.9 us -> 42.9 us  [shards(): probability_mixed_bank = lax.psum(local_weighted, ('bank', 'head'))]
  transfers between devices with their start and end apart: 5 -> 7, of which waited for: 5 -> 5; matrix products, arithmetic and copies ran while one was open for 7% -> 24% of each run, Pallas kernels for 0% -> 0%
where the time goes in v1:
time: 357 us; the launch traced here: 355 us
  waiting for transfers between devices  160 us (45%)
  matrix products  63.2 us (18%)
  local copies, waits for them, and re-layouts  51.8 us (15%)
  blocking collectives  28.9 us (8%)
  loops' own time  21.9 us (6%)
  between operations  14 us (4%)
  other arithmetic  11.7 us (3%)
  starting transfers between devices  4.01 us (1%)
    psum x1, waiting for transfers between devices, shards(): embed = lax.psum(partial_embed, ('bank', 'head'))  54.2 us
    psum x1, waiting for transfers between devices, shards(): probability_mixed_bank = lax.psum(local_weighted, ('bank', 'head'))  42.9 us
    psum x1, waiting for transfers between devices, shards(): grad_second = lax.psum(second_part, 'dp')  35.6 us
    dot_general x16, matrix products, exact_scores(): lax.dot_general(anchor_matrix, bank_entries, (((1,), (1,)), ((), ())), pr...  34.4 us
    dot_general x8, matrix products, second_pass(): jnp.dot(shares, bank_entries, precision=lax.Precision.HIGHEST, preferred_...  23.8 us
    unnamed x27, local copies, waits for them, and re-layouts  20.5 us
    all_gather x2, blocking collectives, joined(): everything = jax.tree.map(lambda part: lax.all_gather(part, axis), array)  16.8 us
    dynamic_slice x16, local copies, waits for them, and re-layouts, block_keys(): return lax.dynamic_slice_in_dim(bank, local_blocks[index] * BLOCK, BLOCK, 0)  15.2 us
  transfers between devices with their start and end apart: 7, of which 5 were waited for; matrix products, arithmetic and copies ran while one was open for 24% of the time, Pallas kernels for 0%

profile of v1, /device:TPU:0, one launch (start us, length us, event | category | flops | bytes accessed | tf_op | source)
XLA Modules:
  0.0 355.2 jit_solution(13630992827867676711)
XLA Ops:
  7.2 4.6 %copy.56 = f32[4096,256]{1,0:T(8,128)} copy(f32[4096,256]{1,0:T(8,128)} %param.17) | data formatting | bytes 8388608
  16.9 54.2 %all-reduce.4.cloned.1.call-done = f32[512,256]{1,0:T(8,128)} async-done(((f32[512,256]{1,0:T(8,128)}), f32[512,256]{1,0:T(8,128)}) %all-reduce.4.cloned.1.call-update) | async-done | bytes 524304 | tf_op jit(solution)/shard_map/psum | solution.py:66
  74.3 34.9 %while.39 = (s32[]{:T(128)}, f32[512]{0:T(512)S(1)}, f32[512]{0:T(512)S(1)}, s32[]{:T(128)}, s32[32]{0:T(128)S(1)}, /*index=5*/f32[4096,256]{1,0:T(8,128)}, f32[...) while((s32[]{:T(128)}, f32[512]{0:T(512)S(1)}, ...), condition=%wide.region_7.8_spmd, body=%wide.region_4.0_spmd.sunk | while | flops 806355968 | bytes 3172573 | solution.py:94
  109.3 7.4 %all-gather.2 = f32[8,1,512]{2,1,0:T(1,128)S(1)} all-gather(f32[1,1,512]{2,1,0:T(1,128)S(1)} %bitcast.48), channel_id=2, replica_groups=mesh['dp'=4,'bank'=4,'head'=2] {'bank','head'}, dimensions={0}, use_global_device_ids=true | all-gather | bytes 18432 | tf_op jit(solution)/shard_map/all_gather | solution.py:26
  116.7 9.4 %all-gather.3 = f32[8,1,512]{2,1,0:T(1,128)S(1)} all-gather(f32[1,1,512]{2,1,0:T(1,128)S(1)} %bitcast.51), channel_id=3, replica_groups=mesh['dp'=4,'bank'=4,'head'=2] {'bank','head'}, dimensions={0}, use_global_device_ids=true | all-gather | bytes 18432 | tf_op jit(solution)/shard_map/all_gather | solution.py:26
  127.5 2.4 collective-permute-start.2
  130.9 12.1 %collective-permute-done = f32[512,256]{1,0:T(8,128)} collective-permute-done((f32[512,256]{1,0:T(8,128)}, f32[512,256]{1,0:T(8,128)}, u32[]{:S(2)}, u32[]{:S(2)}) %collective-permute-start) | collective-permute-done | bytes 524320 | tf_op jit(solution)/shard_map/ppermute | solution.py:18
  143.1 61.9 %while.41 = (s32[]{:T(128)}, f32[512,256]{1,0:T(8,128)S(1)}, s32[]{:T(128)}, s32[32]{0:T(128)}, f32[4096,256]{1,0:T(8,128)}, /*index=5*/f32[512,256]{1,0:T(8,128...) while((s32[]{:T(128)}, f32[512,256]{1,0:T(8,128)S(1)}, ...), condition=%wide.region_13.14_spmd, body=%wide.region_12.13_spmd.sunk | while | flops 1611530240 | bytes 4722921 | solution.py:113
  147.7 3.0 convolution_add_fusion.2
  155.4 3.0 convolution_add_fusion.2
  160.9 2.2 fusion.47
  163.1 3.0 convolution_add_fusion.2
  170.7 3.0 convolution_add_fusion.2
  176.2 2.2 fusion.47
  178.4 3.0 convolution_add_fusion.2
  186.0 3.0 convolution_add_fusion.2
  193.7 3.0 convolution_add_fusion.2
  201.3 3.0 convolution_add_fusion.2
  217.1 42.9 %all-reduce.6.cloned.1.call-done = f32[512,256]{1,0:T(8,128)} async-done(((f32[512,256]{1,0:T(8,128)}), f32[512,256]{1,0:T(8,128)}) %all-reduce.6.cloned.1.call-update) | async-done | bytes 524304 | tf_op jit(solution)/shard_map/psum | solution.py:114
  263.6 2.4 convolution_bitcast_fusion
  266.1 12.1 %all-gather.4 = f32[4,1,512]{2,1,0:T(1,128)S(1)} all-gather(f32[1,1,512]{2,1,0:T(1,128)S(1)} %bitcast.57), channel_id=1, replica_groups=mesh['dp'=4,'bank'=4,'head'=2] {'dp'}, dimensions={0}, use_global_device_ids=true | all-gather | bytes 10240 | tf_op jit(solution)/shard_map/all_gather | solution.py:140
  281.1 13.4 %scatter_custom_fusion = f32[4096,256]{1,0:T(8,128)} fusion(f32[4096,256]{1,0:T(8,128)} %get-tuple-element.546, s32[2048]{0:T(1024)S(1)} %compare_select_fusion, f32[4096,256]{1,0:T(8,128)} %constant_dynamic-update-slice_fusion, s32[]{:T(128)S(6)} %select_n.66, s32[]{:T(128)} %constant.127.clone.1), kind=kCustom, calls=%fused_computation.20 | custom fusion | bytes 6291972 | tf_op jit(solution)/shard_map/scatter | solution.py:144
  294.5 14.9 %reduce-scatter.2.cloned.1.call-done = f32[512,256]{0,1:T(8,128)} async-done(((f32[2048,256]{0,1:T(8,128)}), f32[512,256]{0,1:T(8,128)}) %reduce-scatter.2.cloned.1.call-update) | async-done | bytes 524304 | tf_op jit(solution)/shard_map/reduce_scatter | solution.py:130
  311.4 35.6 %all-reduce.8.cloned.1.call-done = f32[256,256]{1,0:T(8,128)} async-done(((f32[256,256]{1,0:T(8,128)}), f32[256,256]{1,0:T(8,128)}) %all-reduce.8.cloned.1.call-update) | async-done | bytes 262160 | tf_op jit(solution)/shard_map/psum | solution.py:125
  (142 shorter events, 80.2 us)
Async XLA Ops:
  7.2 4.7 %copy-start = (bf16[512,2048]{1,0:T(8,128)(2,1)S(1)}, bf16[512,2048]{1,0:T(8,128)(2,1)}, u32[]{:S(2)}) copy-start(bf16[512,2048]{1,0:T(8,128)(2,1)} %param.13) | copy-start | bytes 6291460
  7.2 5.4 %copy-start.4 = (bf16[256,256]{1,0:T(8,128)(2,1)S(1)}, bf16[256,256]{1,0:T(8,128)(2,1)}, u32[]{:S(2)}) copy-start(bf16[256,256]{1,0:T(8,128)(2,1)} %param.15) | copy-start | bytes 393220
  7.2 63.9 %all-reduce.4.cloned.1.call-start = ((), (), s32[]{:S(2)}) async-start(), calls=%async_computation.1 | async-start | bytes 1048576 | tf_op jit(solution)/shard_map/psum | solution.py:66
  7.2 4.6 %copy-start.7 = (bf16[2048,256]{1,0:T(8,128)(2,1)S(1)}, bf16[2048,256]{1,0:T(8,128)(2,1)}, u32[]{:S(2)}) copy-start(bf16[2048,256]{1,0:T(8,128)(2,1)} %param.14) | copy-start | bytes 3145732
  11.9 1.8 copy-start.1
  11.9 4.9 %copy-start.3 = (f32[512,256]{1,0:T(8,128)S(1)}, f32[512,256]{1,0:T(8,128)}, u32[]{:S(2)}) copy-start(f32[512,256]{1,0:T(8,128)} %param.16) | copy-start | bytes 1572868
  13.7 246.4 %all-reduce.6.cloned.1.call-start = ((), (), s32[]{:S(2)}) async-start(), calls=%async_computation.2 | async-start | bytes 1048576 | tf_op jit(solution)/shard_map/psum | solution.py:114
  109.3 21.0 %copy-start.6 = (s32[32]{0:T(128)}, s32[32]{0:T(128)S(1)}, u32[]{:S(2)}) copy-start(s32[32]{0:T(128)S(1)} %get-tuple-element.557) | copy-start | bytes 388
  126.1 16.9 %collective-permute-start = (f32[512,256]{1,0:T(8,128)}, f32[512,256]{1,0:T(8,128)}, u32[]{:S(2)}, u32[]{:S(2)}) collective-permute-start(f32[512,256]{1,0:T(8,128)} %get-tuple-element.283), channel_id=1, source_target_pairs={{0,8},{8,16},{16,24},{24,0},{1,9},{9,17},{17,25},{25,1},{2,10},{10... | collective-permute-start | bytes 1572872 | tf_op jit(solution)/shard_map/ppermute | solution.py:18
  127.5 84.0 %collective-permute-start.2 = (f32[512,256]{1,0:T(8,128)}, f32[512,256]{1,0:T(8,128)}, u32[]{:S(2)}, u32[]{:S(2)}) collective-permute-start(f32[512,256]{1,0:T(8,128)} %get-tuple-element.283), channel_id=1, source_target_pairs={{0,24},{8,0},{16,8},{24,16},{1,25},{9,1},{17,9},{25,17},{2,26},{10... | collective-permute-start | bytes 1572872 | tf_op jit(solution)/shard_map/ppermute | solution.py:20
  143.0 62.8 %collective-permute-start.1 = (f32[512,256]{1,0:T(8,128)}, f32[512,256]{1,0:T(8,128)}, u32[]{:S(2)}, u32[]{:S(2)}) collective-permute-start(f32[512,256]{1,0:T(8,128)} %collective-permute-done), channel_id=1, source_target_pairs={{0,8},{8,16},{16,24},{24,0},{1,9},{9,17},{17,25},{25,1},{2,10},{10... | collective-permute-start | bytes 1572872 | tf_op jit(solution)/shard_map/ppermute | solution.py:18
  205.0 0.8 copy-start.2
  205.8 103.6 %reduce-scatter.2.cloned.1.call-start = ((), (), s32[]{:S(2)}) async-start(), calls=%async_computation.3 | async-start | bytes 2621440 | tf_op jit(solution)/shard_map/reduce_scatter | solution.py:130
  262.1 4.0 %copy-start.5 = (s32[512]{0:T(512)S(1)}, s32[512]{0:T(512)}, u32[]{:S(2)}) copy-start(s32[512]{0:T(512)} %param.19) | copy-start | bytes 6148
  266.0 81.0 %all-reduce.8.cloned.1.call-start = ((), (), s32[]{:S(2)}) async-start(), calls=%async_computation.4 | async-start | bytes 524288 | tf_op jit(solution)/shard_map/psum | solution.py:125
Sparse Core Ops, SparseCore 0:
  13.8 57.2 all-reduce.3
  205.9 54.0 all-reduce.5
  266.2 43.1 reduce-scatter.1
  312.3 34.6 all-reduce.7
